TPU v7x, 256 devices: a whole 4x4x8 slice. The times are simulated.
256 devices in a mesh: row: 16 (over y, x), col: 8 (over z), vox: 2 (over core).
Axes of the slice: x: 4, y: 4, z: 8, core: 2. Of those that a mesh axis runs over, the one named last changes fastest.
Arguments:
- coeffs_r: bfloat16 [32, 16, 64, 2, 1024], P(None, 'row', None, None, 'col'), may hold values from -0.125 to 0.125
- rhs: bfloat16 [32, 16, 64, 1536], P('col', 'row', None, 'vox'), may hold values from -6 to 6
- inverses: bfloat16 [2, 1024, 1024], replicated, may hold values from -0.1875 to 0.1875
Outputs:
- updated: bfloat16 [32, 16, 64, 1536], P('col', 'row', None, 'vox')
All inputs are finite; a program needn't handle non-finite values.
Results may differ from a plain program's by a relative error of at most 0.0049.
Values may be sent and summed in bfloat16 or wider, within the bound.
A program may use at most 64 MiB of HBM per device.

v0:
```python
import jax
import jax.numpy as jnp
from jax import lax
from jax.sharding import PartitionSpec as P


def spread(value, axis, root):
    mine = lax.axis_index(axis) == root
    return lax.psum(jnp.where(mine, value, jnp.zeros_like(value)), axis)


def solve_block(inverse, rhs_block, col_pos, own_cols):
    solved_all = jnp.dot(inverse, rhs_block, preferred_element_type=jnp.float32).astype(
        jnp.bfloat16
    )
    solved_mine = lax.dynamic_slice_in_dim(solved_all, col_pos * own_cols, own_cols, 0)
    return (solved_all, solved_mine)


def local(coeffs_r, rhs, inverses):
    row_count = lax.axis_size("row")
    col_count = lax.axis_size("col")
    row_pos = lax.axis_index("row")
    col_pos = lax.axis_index("col")
    per_col = rhs.shape[0]
    block_rows = rhs.shape[2]
    voxels = rhs.shape[3]
    cycles = coeffs_r.shape[0]
    own_cols = coeffs_r.shape[4]
    block_order = inverses.shape[1]
    tail_cycles = block_order // (block_rows * row_count)
    owner_col = col_count - 1
    tail_piece = rhs[per_col - tail_cycles :]
    tail_rows = lax.all_gather(tail_piece, "row", axis=1, tiled=True)
    tail_rows = spread(tail_rows, "col", owner_col)
    solved_last, last_mine = solve_block(
        inverses[1], tail_rows.reshape(block_order, voxels), col_pos, own_cols
    )
    panel_rows = coeffs_r[cycles - 2 * tail_cycles : cycles - tail_cycles, 0, :, 1, :]
    panel_rows = panel_rows.reshape(tail_cycles * block_rows, own_cols)
    partial_value = -jnp.dot(panel_rows, last_mine, preferred_element_type=jnp.float32)
    known = rhs[per_col - 2 * tail_cycles : per_col - tail_cycles, 0]
    known = known.reshape(tail_cycles * block_rows, voxels).astype(jnp.float32)
    partial_value = partial_value + jnp.where(col_pos == owner_col, known, jnp.zeros_like(known))
    partial_value = partial_value.reshape(tail_cycles, 1, block_rows, voxels)
    padded = jnp.zeros((tail_cycles, row_count, block_rows, voxels), jnp.float32)
    anchor = jnp.zeros((), jnp.int32)
    padded = lax.dynamic_update_slice(padded, partial_value, (anchor, row_pos, anchor, anchor))
    middle_rhs = lax.psum(padded, ("row", "col")).astype(jnp.bfloat16)
    solved_first, first_mine = solve_block(
        inverses[0], middle_rhs.reshape(block_order, voxels), col_pos, own_cols
    )
    stacked_mine = jnp.stack([first_mine, last_mine])
    removed = lax.psum_scatter(
        jnp.einsum("kprjc,jcv->kprv", coeffs_r, stacked_mine, preferred_element_type=jnp.float32),
        "col",
        scatter_dimension=0,
        tiled=True,
    )
    remaining = (rhs.astype(jnp.float32) - removed).astype(jnp.bfloat16)

    def my_rows(solved):
        shaped = solved.reshape(tail_cycles, row_count, block_rows, voxels)
        return lax.dynamic_slice_in_dim(shaped, row_pos, 1, 1)

    window = jnp.concatenate([my_rows(solved_first), my_rows(solved_last)], 0)
    lower_part = jnp.where(col_pos == owner_col, window, remaining[per_col - 2 * tail_cycles :])
    return jnp.concatenate([remaining[: per_col - 2 * tail_cycles], lower_part], 0)


def solution(mesh):
    placed = (P(None, "row", None, None, "col"), P("col", "row", None, "vox"), P())
    return jax.shard_map(
        local, mesh=mesh, in_specs=placed, out_specs=P("col", "row", None, "vox"), check_vma=False
    )
```

profile of v0, /device:TPU:1, one launch (start us, length us, event | category | flops | bytes accessed | tf_op | source)
XLA Modules:
  0.0 951.8 jit_solution(15609546226498273052)
XLA Ops:
  6.5 0.0 all-gather.2.cloned.1.call-start
  6.5 1.5 slice.28
  8.1 0.0 all-gather.2.cloned.1.call-update
  8.1 0.0 all-reduce.3.cloned.1.call-start
  8.2 53.5 %all-gather.2.cloned.1.call-done = bf16[1,16,64,768]{3,2,0,1:T(8,128)(2,1)} async-done(((bf16[1,1,64,768]{3,2,0,1:T(8,128)(2,1)}), bf16[1,16,64,768]{3,2,0,1:T(8,128)(2,1)}) %all-gather.2.cloned.1.call-update) | async-done | bytes 1572880 | tf_op jit(solution)/shard_map/all_gather | solution.py:34
  61.6 1.3 broadcast_select_fusion
  62.9 0.0 all-reduce.3.cloned.1.call-update
  62.9 0.0 reduce-scatter.2.cloned.1.call-start
  63.0 1.4 slice.23
  64.4 75.1 %all-reduce.3.cloned.1.call-done = bf16[1024,768]{1,0:T(8,128)(2,1)} async-done(((bf16[1024,768]{1,0:T(8,128)(2,1)}), bf16[1024,768]{1,0:T(8,128)(2,1)}) %all-reduce.3.cloned.1.call-update) | async-done | bytes 1572880 | tf_op jit(solution)/shard_map/psum | solution.py:9
  139.5 3.9 fusion.6
  143.4 0.0 copy-start
  143.4 0.8 dynamic-slice_bitcast_fusion.1
  144.3 0.0 copy-start.3
  144.3 0.0 copy-start.5
  144.3 0.3 broadcast_in_dim.9
  144.6 0.0 copy-done
  144.6 0.6 copy-done.3
  145.2 0.0 copy-done.5
  145.2 0.2 fusion.15
  145.5 610.3 %all-reduce.4 = bf16[1,16,64,768]{3,2,1,0:T(8,128)(2,1)} all-reduce(f32[1,16,64,768]{3,2,1,0:T(8,128)S(1)} %fusion.15), channel_id=1, replica_groups=mesh['row'=16,'col'=8,'vox'=2] {'row','col'}, use_global_device_ids=true, to_apply=%region_1.2 | all-reduce | flops 786432 | bytes 4718592 | tf_op jit(solution)/shard_map/psum | solution.py:49
  755.8 0.0 copy-start.2
  755.8 0.0 copy-start.4
  755.8 4.0 fusion.9
  759.8 0.1 dynamic-slice_bitcast_fusion
  759.9 0.0 copy-done.2
  759.9 0.0 copy-done.4
  759.9 3.7 convolution_bitcast_fusion
  763.6 0.0 copy-start.1
  763.6 0.0 reduce-scatter.2.cloned.1.call-update
  763.6 1.4 copy-done.1
  765.0 1.6 copy.26
  766.5 0.7 copy.24
  767.2 0.9 constant_dynamic-slice_fusion
  768.1 175.1 %reduce-scatter.2.cloned.1.call-done = f32[4,1,64,768]{3,2,0,1:T(8,128)} async-done(((f32[32,1,64,768]{3,2,0,1:T(8,128)}), f32[4,1,64,768]{3,2,0,1:T(8,128)}) %reduce-scatter.2.cloned.1.call-update) | async-done | bytes 786448 | tf_op jit(solution)/shard_map/reduce_scatter | solution.py:54
  943.3 1.2 subtract_convert_fusion
  944.5 0.8 maximum_bitcast_fusion.2
  (2 shorter events, 0.0 us)
Async XLA Ops:
  6.5 55.1 %all-gather.2.cloned.1.call-start = ((), (), s32[]{:S(2)}) async-start(), calls=%async_computation.1 | async-start | bytes 1671168 | tf_op jit(solution)/shard_map/all_gather | solution.py:34
  8.1 131.4 %all-reduce.3.cloned.1.call-start = ((), (), s32[]{:S(2)}) async-start(), calls=%async_computation.2 | async-start | bytes 3145728 | tf_op jit(solution)/shard_map/psum | solution.py:9
  62.9 880.4 %reduce-scatter.2.cloned.1.call-start = ((), (), s32[]{:S(2)}) async-start(), calls=%async_computation.3 | async-start | bytes 7077888 | tf_op jit(solution)/shard_map/reduce_scatter | solution.py:54
  143.4 1.2 copy-start
  144.3 1.0 copy-start.3
  144.3 1.0 copy-start.5
  755.8 4.1 copy-start.2
  755.8 4.1 copy-start.4
  763.6 1.4 copy-start.1
Sparse Core Ops, SparseCore 0:
  9.8 51.8 all-gather.1
  64.0 75.4 all-reduce.2
  763.7 179.5 reduce-scatter.1
where the time goes:
time: 952 us
  blocking collectives  610 us (64%)
  waiting for transfers between devices  304 us (32%)
  between operations  13.2 us (1%)
  matrix products  11.8 us (1%)
    psum x1, blocking collectives, local(): middle_rhs = lax.psum(padded, ('row', 'col')).astype(jnp.bfloat16)  610 us
    reduce_scatter x1, waiting for transfers between devices, local(): lax.psum_scatter(jnp.einsum('kprjc,jcv->kprv', coeffs_r, stacked_mine, pr...  175 us
    psum x1, waiting for transfers between devices, spread(): return lax.psum(jnp.where(mine, value, jnp.zeros_like(value)), axis)  75.1 us
    all_gather x1, waiting for transfers between devices, local(): tail_rows = lax.all_gather(tail_piece, 'row', axis=1, tiled=True)  53.5 us
  transfers between devices with their start and end apart: 3, of which 3 were waited for; matrix products, arithmetic and copies ran while one was open for 0% of the time, Pallas kernels for 0%

commit v1 on v0

--- a/solution.py
+++ b/solution.py
@@ -2,6 +2,17 @@
 import jax.numpy as jnp
 from jax import lax
 from jax.sharding import PartitionSpec as P
+
+
+def around_the_ring(x, axis, along):
+    count = lax.axis_size(axis)
+    hops = [(i, (i + 1) % count) for i in range(count)]
+    parts = [x]
+    for far in range(1, count):
+        parts = [lax.ppermute(parts[0], axis, hops), *parts]
+    whole = jnp.concatenate(parts, axis=along)
+    places = (lax.axis_index(axis) + 1) * parts[-1].shape[along]
+    return jnp.roll(whole, places, axis=along)
 
 
 def spread(value, axis, root):
@@ -31,7 +42,7 @@
     tail_cycles = block_order // (block_rows * row_count)
     owner_col = col_count - 1
     tail_piece = rhs[per_col - tail_cycles :]
-    tail_rows = lax.all_gather(tail_piece, "row", axis=1, tiled=True)
+    tail_rows = around_the_ring(tail_piece, "row", 1)
     tail_rows = spread(tail_rows, "col", owner_col)
     solved_last, last_mine = solve_block(
         inverses[1], tail_rows.reshape(block_order, voxels), col_pos, own_cols

time: 952 us -> 1020 us (1.071)
  waiting for transfers between devices: 304 us -> 367 us
    ppermute x0 -> x15, waiting for transfers between devices: none -> 103 us  [around_the_ring(): parts = [lax.ppermute(parts[0], axis, hops), *parts]]
    all_gather x1 -> x0, waiting for transfers between devices: 53.5 us -> none  [local(): tail_rows = lax.all_gather(tail_piece, 'row', axis=1, tiled=True)]
    psum x1, waiting for transfers between devices: 75.1 us -> 88.1 us  [spread(): return lax.psum(jnp.where(mine, value, jnp.zeros_like(value)), axis)]
  transfers between devices with their start and end apart: 3 -> 17, of which waited for: 3 -> 17; matrix products, arithmetic and copies ran while one was open for 0% -> 0% of each run, Pallas kernels for 0% -> 0%
where the time goes in v1:
time: 1020 us
  blocking collectives  610 us (60%)
  waiting for transfers between devices  367 us (36%)
  between operations  13.8 us (1%)
  matrix products  11.8 us (1%)
    psum x1, blocking collectives, local(): middle_rhs = lax.psum(padded, ('row', 'col')).astype(jnp.bfloat16)  610 us
    reduce_scatter x1, waiting for transfers between devices, local(): lax.psum_scatter(jnp.einsum('kprjc,jcv->kprv', coeffs_r, stacked_mine, pr...  176 us
    ppermute x15, waiting for transfers between devices, around_the_ring(): parts = [lax.ppermute(parts[0], axis, hops), *parts]  103 us
    psum x1, waiting for transfers between devices, spread(): return lax.psum(jnp.where(mine, value, jnp.zeros_like(value)), axis)  88.1 us
  transfers between devices with their start and end apart: 17, of which 17 were waited for; matrix products, arithmetic and copies ran while one was open for 0% of the time, Pallas kernels for 0%

profile of v1, /device:TPU:1, one launch (start us, length us, event | category | flops | bytes accessed | tf_op | source)
XLA Modules:
  0.0 1016.6 jit_solution(17057649622156255049)
XLA Ops:
  6.5 0.0 copy-start.3
  6.5 0.0 all-reduce.3.cloned.1.call-start
  6.5 1.0 slice.21
  7.5 2.0 collective-permute-start
  9.5 5.7 collective-permute-done
  15.3 0.0 collective-permute-start.1
  15.3 6.8 collective-permute-done.1
  22.1 0.0 collective-permute-start.2
  22.1 6.8 collective-permute-done.2
  28.8 0.0 collective-permute-start.3
  28.9 6.8 collective-permute-done.3
  35.6 0.0 collective-permute-start.4
  35.6 7.2 collective-permute-done.4
  42.9 0.0 collective-permute-start.5
  42.9 7.6 collective-permute-done.5
  50.4 0.0 collective-permute-start.6
  50.4 6.8 collective-permute-done.6
  57.2 0.0 collective-permute-start.7
  57.2 6.8 collective-permute-done.7
  64.0 0.0 collective-permute-start.8
  64.0 6.8 collective-permute-done.8
  70.8 0.0 collective-permute-start.9
  70.8 6.8 collective-permute-done.9
  77.6 0.0 collective-permute-start.10
  77.6 6.8 collective-permute-done.10
  84.4 0.0 collective-permute-start.11
  84.4 7.1 collective-permute-done.11
  91.4 0.0 collective-permute-start.12
  91.4 7.8 collective-permute-done.12
  99.3 0.0 collective-permute-start.13
  99.3 6.8 collective-permute-done.13
  106.1 0.0 collective-permute-start.14
  106.1 6.8 collective-permute-done.14
  113.1 0.0 copy-done.3
  113.4 1.2 dynamic-slice_select_fusion
  114.6 0.0 all-reduce.3.cloned.1.call-update
  114.7 0.2 reduce-scatter.2.cloned.1.call-start
  114.9 1.4 slice.23
  116.3 88.1 %all-reduce.3.cloned.1.call-done = bf16[1024,768]{1,0:T(8,128)(2,1)} async-done(((bf16[1024,768]{1,0:T(8,128)(2,1)}), bf16[1024,768]{1,0:T(8,128)(2,1)}) %all-reduce.3.cloned.1.call-update) | async-done | bytes 1572880 | tf_op jit(solution)/shard_map/psum | solution.py:20
  204.3 3.9 fusion.6
  208.3 0.0 copy-start
  208.3 0.0 copy-start.5
  208.3 0.8 dynamic-slice_bitcast_fusion.1
  209.1 0.3 broadcast_in_dim.9
  209.4 0.1 copy-done
  209.5 0.0 copy-done.5
  209.5 0.2 fusion.15
  209.7 609.8 %all-reduce.4 = bf16[1,16,64,768]{3,2,1,0:T(8,128)(2,1)} all-reduce(f32[1,16,64,768]{3,2,1,0:T(8,128)S(1)} %fusion.15), channel_id=1, replica_groups=mesh['row'=16,'col'=8,'vox'=2] {'row','col'}, use_global_device_ids=true, to_apply=%region_1.2 | all-reduce | flops 786432 | bytes 4718592 | tf_op jit(solution)/shard_map/psum | solution.py:60
  819.6 0.0 copy-start.2
  819.6 0.0 copy-start.4
  819.6 4.0 fusion.9
  823.6 0.1 dynamic-slice_bitcast_fusion
  823.6 0.0 copy-done.2
  823.6 0.0 copy-done.4
  823.7 3.7 convolution_bitcast_fusion
  827.4 0.0 copy-start.1
  827.4 0.0 reduce-scatter.2.cloned.1.call-update
  827.4 1.4 copy-done.1
  828.8 1.6 copy.16
  830.3 0.7 copy.14
  831.0 0.9 constant_dynamic-slice_fusion
  831.9 175.8 %reduce-scatter.2.cloned.1.call-done = f32[4,1,64,768]{3,2,0,1:T(8,128)} async-done(((f32[32,1,64,768]{3,2,0,1:T(8,128)}), f32[4,1,64,768]{3,2,0,1:T(8,128)}) %reduce-scatter.2.cloned.1.call-update) | async-done | bytes 786448 | tf_op jit(solution)/shard_map/reduce_scatter | solution.py:65
  1007.8 1.2 subtract_convert_fusion
  1009.0 0.8 maximum_bitcast_fusion.2
  (34 shorter events, 0.3 us)
Async XLA Ops:
  6.5 106.6 %copy-start.3 = (bf16[4,1,64,768]{3,2,1,0:T(8,128)(2,1)S(1)}, bf16[4,1,64,768]{3,2,1,0:T(8,128)(2,1)}, u32[]{:S(2)}) copy-start(bf16[4,1,64,768]{3,2,1,0:T(8,128)(2,1)} %param.4) | copy-start | bytes 1179652
  6.5 197.8 %all-reduce.3.cloned.1.call-start = ((), (), s32[]{:S(2)}) async-start(), calls=%async_computation.1 | async-start | bytes 3145728 | tf_op jit(solution)/shard_map/psum | solution.py:20
  7.5 7.8 collective-permute-start
  15.3 6.8 collective-permute-start.1
  22.1 6.8 collective-permute-start.2
  28.8 6.8 collective-permute-start.3
  35.6 7.2 collective-permute-start.4
  42.9 7.6 collective-permute-start.5
  50.4 6.8 collective-permute-start.6
  57.2 6.8 collective-permute-start.7
  64.0 6.8 collective-permute-start.8
  70.8 6.8 collective-permute-start.9
  77.6 6.8 collective-permute-start.10
  84.4 7.1 collective-permute-start.11
  91.4 7.8 collective-permute-start.12
  99.3 6.8 collective-permute-start.13
  106.1 6.8 collective-permute-start.14
  114.7 893.1 %reduce-scatter.2.cloned.1.call-start = ((), (), s32[]{:S(2)}) async-start(), calls=%async_computation.2 | async-start | bytes 7077888 | tf_op jit(solution)/shard_map/reduce_scatter | solution.py:65
  208.3 1.2 copy-start
  208.3 1.2 copy-start.5
  819.6 4.1 copy-start.2
  819.6 4.1 copy-start.4
  827.4 1.4 copy-start.1
Sparse Core Ops, SparseCore 0:
  114.8 89.5 all-reduce.2
  827.5 180.2 reduce-scatter.1
